TPU v7x, 32 devices: a whole 2x2x4 slice. The times are simulated.
32 devices in a mesh: row: 8 (over y, x, core), col: 4 (over z).
Axes of the slice: x: 2, y: 2, z: 4, core: 2. Of those that a mesh axis runs over, the one named last changes fastest.
Arguments:
- matrix: float32 [8192, 2048], P('row', 'col'), may hold values from -100 to 100, as said below
Outputs:
- updated: float32 [8192, 2048], P('row', 'col')
- top: float32 [128, 2048], P(None, 'col')
Inputs may be any that keep to these rules, and one draw needn't show every extreme that they name: The first 128 columns of matrix have full column rank.
All inputs are finite; a program needn't handle non-finite values.
Results may differ from a plain program's by a relative error of at most 0.0006.
Values sent between devices are 32-bit elements; how exact they have to be, the bound alone decides.
A program may use at most 64 MiB of HBM per device.

v0:
```python
import functools
import math

import jax
import jax.numpy as jnp
from jax import lax
from jax.experimental import pallas as pl
from jax.experimental.pallas import tpu as pltpu
from jax.sharding import PartitionSpec as P

B = 128
S = 8
CHUNKS = 8
HI = lax.Precision.HIGHEST


def mm(left, right, dims):
    return lax.dot_general(
        left, right, (dims, ((), ())), precision=HI, preferred_element_type=jnp.float32
    )


def factor_steps(w_ref, low, high):
    lane = lax.broadcasted_iota(jnp.int32, (S, B), 1)
    sub = lax.broadcasted_iota(jnp.int32, (S, B), 0)
    wide = lax.broadcasted_iota(jnp.int32, (B, B), 1)

    def step(k, carry):
        w = w_ref[...]
        rows = w[:S]
        d = {}
        for i in range(S):
            for j in range(i + 1):
                d[i, j] = jnp.broadcast_to(rows[i : i + 1, j : j + 1], (S, B))
        rows = jnp.where(lane < S, jnp.where(lane == sub, 1.0, 0.0), rows)
        p = [jnp.broadcast_to(rows[j : j + 1], (S, B)) for j in range(S)]
        t = None
        for j in range(S):
            inv = lax.rsqrt(d[j, j])
            l = {i: d[i, j] * inv for i in range(j + 1, S)}
            for i in range(j + 1, S):
                for m in range(j + 1, i + 1):
                    d[i, m] = d[i, m] - l[i] * l[m]
            tj = p[j] * inv
            for i in range(j + 1, S):
                p[i] = p[i] - l[i] * tj
            t = tj if t is None else jnp.where(sub == j, tj, t)
        mult = jnp.where((lane >= S) & (lane < B - S * k), t, 0.0)
        t = pltpu.roll(t, B - S, 1)
        rest = pltpu.roll(jnp.where(wide < S, 0.0, w), B - S, 1)
        rest = rest - mm(mult, t, ((0,), (0,)))
        w_ref[: B - S] = rest[S:]
        w_ref[B - S :] = t
        return carry

    lax.fori_loop(low, high, step, 0)


class Sum:
    def __init__(self, size, me, src, box, full, sems):
        self.size, self.me, self.src, self.box, self.full = size, me, src, box, full
        self.sems = sems
        self.slab = max(8, B // size)
        self.owners = B // self.slab

    def rows(self, owner):
        return pl.ds(pl.multiple_of(owner * self.slab, self.slab), self.slab)

    def own(self, device, what):
        if self.owners == self.size:
            what()
        else:
            pl.when(device < self.owners)(what)

    def scatter_copy(self, i):
        peer = self.me ^ i
        return pltpu.make_async_remote_copy(
            src_ref=self.src.at[self.rows(peer)],
            dst_ref=self.box.at[i],
            send_sem=self.sems.at[0, i],
            recv_sem=self.sems.at[1, i],
            device_id={"row": peer},
            device_id_type=pl.DeviceIdType.MESH,
        )

    def scatter_from(self, i):
        return pltpu.make_async_remote_copy(
            src_ref=self.box.at[i],
            dst_ref=self.box.at[i],
            send_sem=self.sems.at[0, i],
            recv_sem=self.sems.at[1, i],
            device_id={"row": self.me ^ i},
            device_id_type=pl.DeviceIdType.MESH,
        )

    def gather_copy(self, i, owner):
        return pltpu.make_async_remote_copy(
            src_ref=self.full.at[self.rows(owner)],
            dst_ref=self.full.at[self.rows(owner)],
            send_sem=self.sems.at[2, i],
            recv_sem=self.sems.at[3, i],
            device_id={"row": self.me ^ i},
            device_id_type=pl.DeviceIdType.MESH,
        )

    def start(self):
        for i in range(1, self.size):
            self.own(self.me ^ i, lambda: self.scatter_copy(i).start())

    def middle(self):
        for i in range(1, self.size):
            self.own(self.me ^ i, lambda: self.scatter_copy(i).wait_send())

        def add():
            total = self.src[self.rows(self.me)]
            for i in range(1, self.size):
                self.scatter_from(i).wait_recv()
                total = total + self.box[i]
            self.full[self.rows(self.me)] = total
            for i in range(1, self.size):
                self.gather_copy(i, self.me).start()

        self.own(self.me, add)

    def end(self):
        for i in range(1, self.size):
            self.own(self.me ^ i, lambda: self.gather_copy(i, self.me ^ i).wait_recv())

    def drain(self):
        def sent():
            for i in range(1, self.size):
                self.gather_copy(i, self.me).wait_send()

        self.own(self.me, sent)


def kernel(
    nrow, ncol, m_hbm, out_hbm, top_ref,
    m_v, a_v, q_v, o_v, s1_v, s2_v, sp_v, g1_v, g2_v, p_v, box1, box2, boxp,
    in_sems, out_sems, chain_sems, g_sems, sems1, sems2, semsp,
):
    me = lax.axis_index("row")
    z = lax.axis_index("col")
    height, width = m_v.shape
    part = height // CHUNKS
    load_m = pltpu.make_async_copy(m_hbm, m_v, in_sems.at[0])
    load_a = pltpu.make_async_copy(m_hbm.at[:, pl.ds(0, B)], a_v, in_sems.at[1])

    @pl.when(z == 0)
    def _():
        load_a.start()

    load_m.start()

    barrier = pltpu.get_barrier_semaphore()
    for i in range(1, nrow):
        pl.semaphore_signal(
            barrier, inc=1, device_id={"row": me ^ i}, device_id_type=pl.DeviceIdType.MESH
        )
    for i in range(1, ncol):
        pl.semaphore_signal(
            barrier, inc=1, device_id={"col": z ^ i}, device_id_type=pl.DeviceIdType.MESH
        )

    @pl.when(z == 0)
    def _():
        load_a.wait()
        s1_v[...] = mm(a_v[...], a_v[...], ((0,), (0,)))

    pl.semaphore_wait(barrier, nrow + ncol - 2)

    def chain(c):
        block = a_v.at[pl.ds(c * part, part)]
        return pltpu.make_async_remote_copy(
            src_ref=block,
            dst_ref=block,
            send_sem=chain_sems.at[0, c],
            recv_sem=chain_sems.at[1, c],
            device_id={"col": lax.rem(z + 1, ncol)},
            device_id_type=pl.DeviceIdType.MESH,
        )

    def hand(i):
        return pltpu.make_async_remote_copy(
            src_ref=g1_v,
            dst_ref=g1_v,
            send_sem=g_sems.at[0, i],
            recv_sem=g_sems.at[1, 0],
            device_id={"col": i},
            device_id_type=pl.DeviceIdType.MESH,
        )

    @pl.when(z == 0)
    def _():
        first = Sum(nrow, me, s1_v, box1, g1_v, sems1)
        first.start()
        for c in range(CHUNKS):
            chain(c).start()
        first.middle()
        first.end()
        first.drain()
        factor_steps(g1_v, 0, B // S)
        for i in range(1, ncol):
            hand(i).start()

    @pl.when(z > 0)
    def _():
        for c in range(CHUNKS):
            chain(c).wait_recv()

            @pl.when(z < ncol - 1)
            def _():
                chain(c).start()

        hand(0).wait_recv()

    load_m.wait()
    for c in range(CHUNKS):
        rows = pl.ds(c * part, part)
        q_v[rows] = mm(a_v[rows], g1_v[...], ((1,), (1,)))
    q = q_v[...]
    s2_v[...] = mm(q, q, ((0,), (0,)))
    second = Sum(nrow, me, s2_v, box2, g2_v, sems2)
    second.start()
    coeffs = Sum(nrow, me, sp_v, boxp, p_v, semsp)
    sp_v[...] = mm(q_v[...], m_v[...], ((0,), (0,)))
    coeffs.start()
    second.middle()
    second.end()
    second.drain()
    factor_steps(g2_v, 0, B // S // 2)
    coeffs.middle()
    factor_steps(g2_v, B // S // 2, B // S)
    coeffs.end()
    coeffs.drain()

    scale = math.sqrt(height * nrow)
    g2 = g2_v[...]
    on_panel = z == 0
    for c in range(width // B):
        cols = pl.ds(c * B, B)
        part_c = mm(g2, p_v[:, cols], ((1,), (0,)))
        top_ref[:, cols] = part_c / scale
        back = mm(g2, part_c, ((0,), (0,)))
        if c == 0:
            back = jnp.where(on_panel, -scale * g2.T, back)
        p_v[:, cols] = back

    def store(c):
        rows = pl.ds(c * part, part)
        return pltpu.make_async_copy(o_v.at[rows], out_hbm.at[rows], out_sems.at[c])

    for c in range(CHUNKS):
        rows = pl.ds(c * part, part)
        change = mm(q_v[rows], p_v[...], ((1,), (0,)))
        base = m_v[rows]
        o_v[rows, :B] = jnp.where(on_panel, 0.0, base[:, :B]) - change[:, :B]
        o_v[rows, B:] = base[:, B:] - change[:, B:]
        store(c).start()
    for c in range(CHUNKS):
        store(c).wait()

    @pl.when(z < ncol - 1)
    def _():
        for c in range(CHUNKS):
            chain(c).wait_send()

    @pl.when(z == 0)
    def _():
        for i in range(1, ncol):
            hand(i).wait_send()


def on_device(nrow, ncol, matrix):
    height, width = matrix.shape
    slab = max(8, B // nrow)
    f32 = jnp.float32
    dma = pltpu.SemaphoreType.DMA
    return pl.pallas_call(
        functools.partial(kernel, nrow, ncol),
        out_shape=(
            jax.ShapeDtypeStruct((height, width), f32),
            jax.ShapeDtypeStruct((B, width), f32),
        ),
        in_specs=[pl.BlockSpec(memory_space=pl.ANY)],
        out_specs=(
            pl.BlockSpec(memory_space=pl.ANY),
            pl.BlockSpec(memory_space=pltpu.VMEM),
        ),
        scratch_shapes=[
            pltpu.VMEM((height, width), f32),
            pltpu.VMEM((height, B), f32),
            pltpu.VMEM((height, B), f32),
            pltpu.VMEM((height, width), f32),
            pltpu.VMEM((B, B), f32),
            pltpu.VMEM((B, B), f32),
            pltpu.VMEM((B, width), f32),
            pltpu.VMEM((B, B), f32),
            pltpu.VMEM((B, B), f32),
            pltpu.VMEM((B, width), f32),
            pltpu.VMEM((nrow, slab, B), f32),
            pltpu.VMEM((nrow, slab, B), f32),
            pltpu.VMEM((nrow, slab, width), f32),
            dma((2,)),
            dma((CHUNKS,)),
            dma((2, CHUNKS)),
            dma((2, ncol)),
            dma((4, nrow)),
            dma((4, nrow)),
            dma((4, nrow)),
        ],
        compiler_params=pltpu.CompilerParams(
            collective_id=0, has_side_effects=True, vmem_limit_bytes=40 * 2**20
        ),
    )(matrix)


def solution(mesh):
    nrow, ncol = mesh.shape["row"], mesh.shape["col"]
    return jax.shard_map(
        functools.partial(on_device, nrow, ncol),
        mesh=mesh,
        in_specs=(P("row", "col"),),
        out_specs=(P("row", "col"), P(None, "col")),
        check_vma=False,
    )
```

profile of v0, /device:TPU:25, one launch (start us, length us, event | category | flops | bytes accessed | tf_op | source)
XLA Modules:
  0.0 50.6 jit_solution(17781641141231283882)
XLA Ops:
  0.6 0.0 copy-start
  0.6 1.6 %copy-done = f32[1024,512]{1,0:T(8,128)S(1)} copy-done((f32[1024,512]{1,0:T(8,128)S(1)}, f32[1024,512]{1,0:T(8,128)}, u32[]{:S(2)}) %copy-start) | copy-done | bytes 2097176
  2.2 46.3 %shard_map.30 = (f32[1024,512]{1,0:T(8,128)S(1)}, f32[128,512]{1,0:T(8,128)S(1)}) custom-call(f32[1024,512]{1,0:T(8,128)S(1)} %copy-done), custom_call_target="tpu_custom_call" | custom-call | tf_op jit(solution)/shard_map/pallas_call | solution.py:279
  48.6 1.3 %copy.5 = f32[1024,512]{1,0:T(8,128)} copy(f32[1024,512]{1,0:T(8,128)S(1)} %get-tuple-element.4) | data formatting | bytes 4194304
  49.9 0.7 %copy.6 = f32[128,512]{1,0:T(8,128)} copy(f32[128,512]{1,0:T(8,128)S(1)} %get-tuple-element.5) | data formatting | bytes 524288
Async XLA Ops:
  0.6 1.6 %copy-start = (f32[1024,512]{1,0:T(8,128)S(1)}, f32[1024,512]{1,0:T(8,128)}, u32[]{:S(2)}) copy-start(f32[1024,512]{1,0:T(8,128)} %m_hbm.1) | copy-start | bytes 6291460
where the time goes:
time: 50.7 us; the launch traced here: 50.6 us
  Pallas kernels  46.3 us (91%)
  local copies, waits for them, and re-layouts  3.61 us (7%)
  between operations  0.65 us (1%)
    pallas_call x1, Pallas kernels, on_device(): pl.pallas_call(functools.partial(kernel, nrow, ncol), out_shape=(jax.Shap...  46.3 us
    unnamed x4, local copies, waits for them, and re-layouts  3.61 us

commit v1 on v0

--- a/solution.py
+++ b/solution.py
@@ -20,18 +20,22 @@
     )
 
 
-def factor_steps(w_ref, low, high):
+def factor_steps(w_ref, low, high, state=None):
     lane = lax.broadcasted_iota(jnp.int32, (S, B), 1)
     sub = lax.broadcasted_iota(jnp.int32, (S, B), 0)
-    wide = lax.broadcasted_iota(jnp.int32, (B, B), 1)
-
-    def step(k, carry):
-        w = w_ref[...]
-        rows = w[:S]
+    wide = lax.broadcasted_iota(jnp.int32, (B - 2 * S, B), 1)
+
+    def step(k, state):
+        rows, mult, last = state
         d = {}
-        for i in range(S):
-            for j in range(i + 1):
-                d[i, j] = jnp.broadcast_to(rows[i : i + 1, j : j + 1], (S, B))
+        for j in range(S):
+            column = jnp.broadcast_to(rows[:, j : j + 1], (S, B))
+            for i in range(j, S):
+                d[i, j] = jnp.broadcast_to(column[i : i + 1], (S, B))
+        rest = w_ref[S : B - S] - mm(mult, last, ((0,), (0,)))[2 * S :]
+        rest = pltpu.roll(jnp.where(wide < S, 0.0, rest), B - S, 1)
+        w_ref[: B - 2 * S] = rest
+        w_ref[B - 2 * S : B - S] = pltpu.roll(jnp.where(lane < S, 0.0, last), B - S, 1)
         rows = jnp.where(lane < S, jnp.where(lane == sub, 1.0, 0.0), rows)
         p = [jnp.broadcast_to(rows[j : j + 1], (S, B)) for j in range(S)]
         t = None
@@ -46,14 +50,20 @@
                 p[i] = p[i] - l[i] * tj
             t = tj if t is None else jnp.where(sub == j, tj, t)
         mult = jnp.where((lane >= S) & (lane < B - S * k), t, 0.0)
-        t = pltpu.roll(t, B - S, 1)
-        rest = pltpu.roll(jnp.where(wide < S, 0.0, w), B - S, 1)
-        rest = rest - mm(mult, t, ((0,), (0,)))
-        w_ref[: B - S] = rest[S:]
-        w_ref[B - S :] = t
-        return carry
-
-    lax.fori_loop(low, high, step, 0)
+        last = pltpu.roll(t, B - S, 1)
+        after = rest[:S]
+        for i in range(S):
+            column = jnp.broadcast_to(mult[:, S + i : S + i + 1], (S, B))
+            drop = jnp.sum(column * last, axis=0, keepdims=True)
+            after = jnp.where(sub == i, after - drop, after)
+        return after, mult, last
+
+    if low == 0:
+        state = (w_ref[:S], jnp.zeros((S, B), jnp.float32), w_ref[B - S :])
+    state = lax.fori_loop(low, high, step, state)
+    if high == B // S:
+        w_ref[B - S :] = state[2]
+    return state
 
 
 class Sum:
@@ -117,10 +127,15 @@
                 self.scatter_from(i).wait_recv()
                 total = total + self.box[i]
             self.full[self.rows(self.me)] = total
+
+        self.own(self.me, add)
+
+    def spread(self):
+        def send():
             for i in range(1, self.size):
                 self.gather_copy(i, self.me).start()
 
-        self.own(self.me, add)
+        self.own(self.me, send)
 
     def end(self):
         for i in range(1, self.size):
@@ -135,22 +150,16 @@
 
 
 def kernel(
-    nrow, ncol, m_hbm, out_hbm, top_ref,
-    m_v, a_v, q_v, o_v, s1_v, s2_v, sp_v, g1_v, g2_v, p_v, box1, box2, boxp,
-    in_sems, out_sems, chain_sems, g_sems, sems1, sems2, semsp,
+    nrow, ncol, m_hbm, q_v, g2_v, p_v,
+    m_v, a_v, s1_v, s2_v, sp_v, g1_v, box1, box2, boxp,
+    in_sems, chain_sems, g_sems, sems1, sems2, semsp,
 ):
     me = lax.axis_index("row")
     z = lax.axis_index("col")
-    height, width = m_v.shape
+    height = m_v.shape[0]
     part = height // CHUNKS
     load_m = pltpu.make_async_copy(m_hbm, m_v, in_sems.at[0])
     load_a = pltpu.make_async_copy(m_hbm.at[:, pl.ds(0, B)], a_v, in_sems.at[1])
-
-    @pl.when(z == 0)
-    def _():
-        load_a.start()
-
-    load_m.start()
 
     barrier = pltpu.get_barrier_semaphore()
     for i in range(1, nrow):
@@ -164,9 +173,11 @@
 
     @pl.when(z == 0)
     def _():
+        load_a.start()
         load_a.wait()
         s1_v[...] = mm(a_v[...], a_v[...], ((0,), (0,)))
 
+    load_m.start()
     pl.semaphore_wait(barrier, nrow + ncol - 2)
 
     def chain(c):
@@ -180,10 +191,17 @@
             device_id_type=pl.DeviceIdType.MESH,
         )
 
+    def forward(c):
+        chain(c).wait_recv()
+        pl.when(z < ncol - 1)(lambda: chain(c).start())
+
+    first = Sum(nrow, me, s1_v, box1, g1_v, sems1)
+    slab = g1_v.at[first.rows(me)]
+
     def hand(i):
         return pltpu.make_async_remote_copy(
-            src_ref=g1_v,
-            dst_ref=g1_v,
+            src_ref=slab,
+            dst_ref=slab,
             send_sem=g_sems.at[0, i],
             recv_sem=g_sems.at[1, 0],
             device_id={"col": i},
@@ -192,29 +210,43 @@
 
     @pl.when(z == 0)
     def _():
-        first = Sum(nrow, me, s1_v, box1, g1_v, sems1)
         first.start()
-        for c in range(CHUNKS):
+        for c in range(2):
             chain(c).start()
         first.middle()
-        first.end()
-        first.drain()
-        factor_steps(g1_v, 0, B // S)
-        for i in range(1, ncol):
-            hand(i).start()
+
+        def give():
+            for i in range(1, ncol):
+                hand(i).start()
+
+        first.own(me, give)
+        for c in range(2, CHUNKS):
+            chain(c).start()
 
     @pl.when(z > 0)
     def _():
-        for c in range(CHUNKS):
-            chain(c).wait_recv()
-
-            @pl.when(z < ncol - 1)
-            def _():
-                chain(c).start()
-
-        hand(0).wait_recv()
-
-    load_m.wait()
+        forward(0)
+        forward(1)
+        first.own(me, lambda: hand(0).wait_recv())
+
+    first.spread()
+    first.end()
+    first.drain()
+
+    @pl.when(z == 0)
+    def _():
+        def given():
+            for i in range(1, ncol):
+                hand(i).wait_send()
+
+        first.own(me, given)
+
+    state = None
+    for low, chunks in ((0, (2, 3)), (4, (4, 5)), (8, (6, 7)), (12, ())):
+        state = factor_steps(g1_v, low, low + 4, state)
+        for c in chunks:
+            pl.when(z > 0)(functools.partial(forward, c))
+
     for c in range(CHUNKS):
         rows = pl.ds(c * part, part)
         q_v[rows] = mm(a_v[rows], g1_v[...], ((1,), (1,)))
@@ -222,53 +254,45 @@
     s2_v[...] = mm(q, q, ((0,), (0,)))
     second = Sum(nrow, me, s2_v, box2, g2_v, sems2)
     second.start()
+    load_m.wait()
     coeffs = Sum(nrow, me, sp_v, boxp, p_v, semsp)
     sp_v[...] = mm(q_v[...], m_v[...], ((0,), (0,)))
     coeffs.start()
     second.middle()
+    second.spread()
     second.end()
     second.drain()
-    factor_steps(g2_v, 0, B // S // 2)
+    state = factor_steps(g2_v, 0, B // S // 2)
     coeffs.middle()
-    factor_steps(g2_v, B // S // 2, B // S)
+    coeffs.spread()
+    factor_steps(g2_v, B // S // 2, B // S, state)
     coeffs.end()
     coeffs.drain()
 
-    scale = math.sqrt(height * nrow)
-    g2 = g2_v[...]
-    on_panel = z == 0
-    for c in range(width // B):
-        cols = pl.ds(c * B, B)
-        part_c = mm(g2, p_v[:, cols], ((1,), (0,)))
-        top_ref[:, cols] = part_c / scale
-        back = mm(g2, part_c, ((0,), (0,)))
-        if c == 0:
-            back = jnp.where(on_panel, -scale * g2.T, back)
-        p_v[:, cols] = back
-
-    def store(c):
-        rows = pl.ds(c * part, part)
-        return pltpu.make_async_copy(o_v.at[rows], out_hbm.at[rows], out_sems.at[c])
-
-    for c in range(CHUNKS):
-        rows = pl.ds(c * part, part)
-        change = mm(q_v[rows], p_v[...], ((1,), (0,)))
-        base = m_v[rows]
-        o_v[rows, :B] = jnp.where(on_panel, 0.0, base[:, :B]) - change[:, :B]
-        o_v[rows, B:] = base[:, B:] - change[:, B:]
-        store(c).start()
-    for c in range(CHUNKS):
-        store(c).wait()
-
     @pl.when(z < ncol - 1)
     def _():
         for c in range(CHUNKS):
             chain(c).wait_send()
 
-    @pl.when(z == 0)
-    def _():
-        for i in range(1, ncol):
-            hand(i).wait_send()
+
+def project_kernel(rows, m_ref, q_ref, g2_ref, p_ref, out_ref, top_ref, back_v):
+    width = m_ref.shape[1]
+    scale = math.sqrt(rows)
+    on_panel = lax.axis_index("col") == 0
+
+    @pl.when(pl.program_id(0) == 0)
+    def _():
+        g2 = g2_ref[...]
+        c = mm(g2, p_ref[...], ((1,), (0,)))
+        top_ref[...] = c / scale
+        back = mm(g2, c, ((0,), (0,)))
+        back_v[:, :B] = jnp.where(on_panel, -scale * g2.T, back[:, :B])
+        back_v[:, B:] = back[:, B:]
+
+    change = mm(q_ref[...], back_v[...], ((1,), (0,)))
+    base = m_ref[...]
+    out_ref[:, :B] = jnp.where(on_panel, 0.0, base[:, :B]) - change[:, :B]
+    out_ref[:, B:] = base[:, B:] - change[:, B:]
 
 
 def on_device(nrow, ncol, matrix):
@@ -276,33 +300,23 @@
     slab = max(8, B // nrow)
     f32 = jnp.float32
     dma = pltpu.SemaphoreType.DMA
-    return pl.pallas_call(
+    shape = jax.ShapeDtypeStruct
+    basis, inverse, coeffs = pl.pallas_call(
         functools.partial(kernel, nrow, ncol),
-        out_shape=(
-            jax.ShapeDtypeStruct((height, width), f32),
-            jax.ShapeDtypeStruct((B, width), f32),
-        ),
+        out_shape=(shape((height, B), f32), shape((B, B), f32), shape((B, width), f32)),
         in_specs=[pl.BlockSpec(memory_space=pl.ANY)],
-        out_specs=(
-            pl.BlockSpec(memory_space=pl.ANY),
-            pl.BlockSpec(memory_space=pltpu.VMEM),
-        ),
+        out_specs=(pl.BlockSpec(memory_space=pltpu.VMEM),) * 3,
         scratch_shapes=[
             pltpu.VMEM((height, width), f32),
             pltpu.VMEM((height, B), f32),
-            pltpu.VMEM((height, B), f32),
-            pltpu.VMEM((height, width), f32),
             pltpu.VMEM((B, B), f32),
             pltpu.VMEM((B, B), f32),
             pltpu.VMEM((B, width), f32),
             pltpu.VMEM((B, B), f32),
-            pltpu.VMEM((B, B), f32),
-            pltpu.VMEM((B, width), f32),
             pltpu.VMEM((nrow, slab, B), f32),
             pltpu.VMEM((nrow, slab, B), f32),
             pltpu.VMEM((nrow, slab, width), f32),
             dma((2,)),
-            dma((CHUNKS,)),
             dma((2, CHUNKS)),
             dma((2, ncol)),
             dma((4, nrow)),
@@ -310,9 +324,28 @@
             dma((4, nrow)),
         ],
         compiler_params=pltpu.CompilerParams(
-            collective_id=0, has_side_effects=True, vmem_limit_bytes=40 * 2**20
+            collective_id=0, has_side_effects=True, vmem_limit_bytes=60 * 2**20
         ),
     )(matrix)
+    part = height // 4
+    whole = pl.BlockSpec(memory_space=pltpu.VMEM)
+    return pl.pallas_call(
+        functools.partial(project_kernel, height * nrow),
+        grid=(height // part,),
+        out_shape=(shape((height, width), f32), shape((B, width), f32)),
+        in_specs=[
+            pl.BlockSpec((part, width), lambda i: (i, 0)),
+            pl.BlockSpec((part, B), lambda i: (i, 0)),
+            whole,
+            whole,
+        ],
+        out_specs=(
+            pl.BlockSpec((part, width), lambda i: (i, 0)),
+            pl.BlockSpec((B, width), lambda i: (0, 0)),
+        ),
+        scratch_shapes=[pltpu.VMEM((B, width), f32)],
+        compiler_params=pltpu.CompilerParams(vmem_limit_bytes=60 * 2**20),
+    )(matrix, basis, inverse, coeffs)
 
 
 def solution(mesh):

time: 50.7 us -> 54 us (1.065)
  Pallas kernels: 46.3 us -> 53.1 us
  local copies, waits for them, and re-layouts: 3.61 us -> 0 us
    pallas_call x1 -> x2, Pallas kernels: 46.3 us -> 53.1 us  [the longest x1 47.3 us: on_device(): pl.pallas_call(functools.partial(kernel, nrow, ncol), out_shape=(shape((h...]
    unnamed x4 -> x0, local copies, waits for them, and re-layouts: 3.61 us -> none
where the time goes in v1:
time: 54 us; the launch traced here: 53.7 us
  Pallas kernels  53.1 us (98%)
  between operations  0.64 us (1%)
    pallas_call x1, Pallas kernels, on_device(): pl.pallas_call(functools.partial(kernel, nrow, ncol), out_shape=(shape((h...  47.3 us
    pallas_call x1, Pallas kernels, on_device(): pl.pallas_call(functools.partial(project_kernel, height * nrow), grid=(he...  5.77 us

profile of v1, /device:TPU:25, one launch (start us, length us, event | category | flops | bytes accessed | tf_op | source)
XLA Modules:
  0.0 53.7 jit_solution(14552836114274518251)
XLA Ops:
  0.6 47.3 %shard_map.30 = (f32[1024,128]{1,0:T(8,128)}, f32[128,128]{1,0:T(8,128)}, f32[128,512]{1,0:T(8,128)}) custom-call(f32[1024,512]{1,0:T(8,128)} %m_ref.1), custom_call_target="tpu_custom_call" | custom-call | tf_op jit(solution)/shard_map/pallas_call | solution.py:304
  48.0 5.8 %shard_map.31 = (f32[1024,512]{1,0:T(8,128)}, f32[128,512]{1,0:T(8,128)}) custom-call(f32[1024,512]{1,0:T(8,128)} %m_ref.1, f32[1024,128]{1,0:T(8,128)} %get-tuple-element.5.q_ref, f32[128,128]{1,0:T(8,128)} %get-tuple-element.6.g2_ref, f32[128,512]{1,0:T(8,128)} %get-tuple-element.7.p_ref), custom_call_target="tpu_custom_call" | custom-call | tf_op jit(solution)/shard_map/pallas_call | solution.py:332

commit v2 on v1

--- a/solution.py
+++ b/solution.py
@@ -20,7 +20,7 @@
     )
 
 
-def factor_steps(w_ref, low, high, state=None):
+def factor_steps(w_ref, low, high, state=None, after_step=None):
     lane = lax.broadcasted_iota(jnp.int32, (S, B), 1)
     sub = lax.broadcasted_iota(jnp.int32, (S, B), 0)
     wide = lax.broadcasted_iota(jnp.int32, (B - 2 * S, B), 1)
@@ -56,6 +56,8 @@
             column = jnp.broadcast_to(mult[:, S + i : S + i + 1], (S, B))
             drop = jnp.sum(column * last, axis=0, keepdims=True)
             after = jnp.where(sub == i, after - drop, after)
+        if after_step is not None:
+            after_step(k)
         return after, mult, last
 
     if low == 0:
@@ -127,6 +129,7 @@
                 self.scatter_from(i).wait_recv()
                 total = total + self.box[i]
             self.full[self.rows(self.me)] = total
+            self.box[0] = total
 
         self.own(self.me, add)
 
@@ -171,17 +174,12 @@
             barrier, inc=1, device_id={"col": z ^ i}, device_id_type=pl.DeviceIdType.MESH
         )
 
-    @pl.when(z == 0)
-    def _():
-        load_a.start()
-        load_a.wait()
-        s1_v[...] = mm(a_v[...], a_v[...], ((0,), (0,)))
-
+    pl.when(z == 0)(load_a.start)
     load_m.start()
     pl.semaphore_wait(barrier, nrow + ncol - 2)
 
     def chain(c):
-        block = a_v.at[pl.ds(c * part, part)]
+        block = a_v.at[pl.ds(pl.multiple_of(c * part, part), part)]
         return pltpu.make_async_remote_copy(
             src_ref=block,
             dst_ref=block,
@@ -191,75 +189,105 @@
             device_id_type=pl.DeviceIdType.MESH,
         )
 
+    passes_on = (z > 0) & (z < ncol - 1)
+
     def forward(c):
         chain(c).wait_recv()
-        pl.when(z < ncol - 1)(lambda: chain(c).start())
+        chain(c).start()
 
     first = Sum(nrow, me, s1_v, box1, g1_v, sems1)
-    slab = g1_v.at[first.rows(me)]
-
-    def hand(i):
+    second = Sum(nrow, me, s2_v, box2, g2_v, sems2)
+    coeffs = Sum(nrow, me, sp_v, boxp, p_v, semsp)
+
+    def hand(which, total, i):
         return pltpu.make_async_remote_copy(
-            src_ref=slab,
-            dst_ref=slab,
-            send_sem=g_sems.at[0, i],
-            recv_sem=g_sems.at[1, 0],
+            src_ref=total.box.at[0],
+            dst_ref=total.full.at[total.rows(me)],
+            send_sem=g_sems.at[2 * which, i],
+            recv_sem=g_sems.at[2 * which + 1, 0],
             device_id={"col": i},
             device_id_type=pl.DeviceIdType.MESH,
         )
 
+    def give(which, total):
+        def send():
+            for i in range(1, ncol):
+                hand(which, total, i).start()
+
+        first.own(me, send)
+
     @pl.when(z == 0)
     def _():
+        load_a.wait()
+        for c in range(3):
+            chain(c).start()
+        s1_v[...] = mm(a_v[...], a_v[...], ((0,), (0,)))
         first.start()
-        for c in range(2):
+        first.middle()
+        give(0, first)
+        first.spread()
+        for c in range(3, CHUNKS):
             chain(c).start()
-        first.middle()
-
-        def give():
-            for i in range(1, ncol):
-                hand(i).start()
-
-        first.own(me, give)
-        for c in range(2, CHUNKS):
-            chain(c).start()
+
+    @pl.when(passes_on)
+    def _():
+        for c in range(4):
+            forward(c)
 
     @pl.when(z > 0)
     def _():
-        forward(0)
-        forward(1)
-        first.own(me, lambda: hand(0).wait_recv())
-
-    first.spread()
+        first.own(me, lambda: hand(0, first, 0).wait_recv())
+        first.spread()
+
     first.end()
     first.drain()
 
+    def pass_on(k):
+        @pl.when(passes_on & (k % 3 == 1) & (k < 12))
+        def _():
+            forward(4 + k // 3)
+
+    factor_steps(g1_v, 0, B // S, None, pass_on)
+
+    big = 2 * part
+
     @pl.when(z == 0)
     def _():
-        def given():
-            for i in range(1, ncol):
-                hand(i).wait_send()
-
-        first.own(me, given)
-
-    state = None
-    for low, chunks in ((0, (2, 3)), (4, (4, 5)), (8, (6, 7)), (12, ())):
-        state = factor_steps(g1_v, low, low + 4, state)
-        for c in chunks:
-            pl.when(z > 0)(functools.partial(forward, c))
-
-    for c in range(CHUNKS):
-        rows = pl.ds(c * part, part)
-        q_v[rows] = mm(a_v[rows], g1_v[...], ((1,), (1,)))
-    q = q_v[...]
-    s2_v[...] = mm(q, q, ((0,), (0,)))
-    second = Sum(nrow, me, s2_v, box2, g2_v, sems2)
-    second.start()
-    load_m.wait()
-    coeffs = Sum(nrow, me, sp_v, boxp, p_v, semsp)
-    sp_v[...] = mm(q_v[...], m_v[...], ((0,), (0,)))
-    coeffs.start()
-    second.middle()
-    second.spread()
+        for c in range(CHUNKS // 2):
+            rows = pl.ds(c * big, big)
+            q_v[rows] = mm(a_v[rows], g1_v[...], ((1,), (1,)))
+        q = q_v[...]
+        s2_v[...] = mm(q, q, ((0,), (0,)))
+        second.start()
+        load_m.wait()
+        sp_v[...] = mm(q_v[...], m_v[...], ((0,), (0,)))
+        second.middle()
+        give(1, second)
+        second.spread()
+        coeffs.start()
+
+    @pl.when(z > 0)
+    def _():
+        load_m.wait()
+        for c in range(CHUNKS // 2):
+
+            @pl.when(z == ncol - 1)
+            def _():
+                chain(2 * c).wait_recv()
+                chain(2 * c + 1).wait_recv()
+
+            rows = pl.ds(c * big, big)
+            q = mm(a_v[rows], g1_v[...], ((1,), (1,)))
+            q_v[rows] = q
+            term = mm(q, m_v[rows], ((0,), (0,)))
+            if c == 0:
+                sp_v[...] = term
+            else:
+                sp_v[...] += term
+        coeffs.start()
+        second.own(me, lambda: hand(1, second, 0).wait_recv())
+        second.spread()
+
     second.end()
     second.drain()
     state = factor_steps(g2_v, 0, B // S // 2)
@@ -269,10 +297,24 @@
     coeffs.end()
     coeffs.drain()
 
+    @pl.when(z == 0)
+    def _():
+        def given():
+            for i in range(1, ncol):
+                hand(0, first, i).wait_send()
+                hand(1, second, i).wait_send()
+
+        first.own(me, given)
+
     @pl.when(z < ncol - 1)
     def _():
         for c in range(CHUNKS):
             chain(c).wait_send()
+
+
+def halves(x):
+    high = x.astype(jnp.bfloat16)
+    return high, (x - high.astype(jnp.float32)).astype(jnp.bfloat16)
 
 
 def project_kernel(rows, m_ref, q_ref, g2_ref, p_ref, out_ref, top_ref, back_v):
@@ -286,10 +328,16 @@
         c = mm(g2, p_ref[...], ((1,), (0,)))
         top_ref[...] = c / scale
         back = mm(g2, c, ((0,), (0,)))
-        back_v[:, :B] = jnp.where(on_panel, -scale * g2.T, back[:, :B])
-        back_v[:, B:] = back[:, B:]
-
-    change = mm(q_ref[...], back_v[...], ((1,), (0,)))
+        leading = jnp.where(on_panel, -scale * g2.T, back[:, :B])
+        high, low = halves(jnp.concatenate([leading, back[:, B:]], 1))
+        back_v[:B] = high
+        back_v[B : 2 * B] = high
+        back_v[2 * B :] = low
+
+    high, low = halves(q_ref[...])
+    change = jnp.dot(
+        jnp.concatenate([high, low, high], 1), back_v[...], preferred_element_type=jnp.float32
+    )
     base = m_ref[...]
     out_ref[:, :B] = jnp.where(on_panel, 0.0, base[:, :B]) - change[:, :B]
     out_ref[:, B:] = base[:, B:] - change[:, B:]
@@ -318,7 +366,7 @@
             pltpu.VMEM((nrow, slab, width), f32),
             dma((2,)),
             dma((2, CHUNKS)),
-            dma((2, ncol)),
+            dma((4, ncol)),
             dma((4, nrow)),
             dma((4, nrow)),
             dma((4, nrow)),
@@ -343,7 +391,7 @@
             pl.BlockSpec((part, width), lambda i: (i, 0)),
             pl.BlockSpec((B, width), lambda i: (0, 0)),
         ),
-        scratch_shapes=[pltpu.VMEM((B, width), f32)],
+        scratch_shapes=[pltpu.VMEM((3 * B, width), jnp.bfloat16)],
         compiler_params=pltpu.CompilerParams(vmem_limit_bytes=60 * 2**20),
     )(matrix, basis, inverse, coeffs)
 

time: 54 us -> 49.4 us (0.915); the launches traced: 53.7 us -> 48.5 us
  Pallas kernels: 53.1 us -> 47.9 us
    pallas_call x1, Pallas kernels: 47.3 us -> 42.7 us  [on_device(): pl.pallas_call(functools.partial(kernel, nrow, ncol), out_shape=(shape((h...]
    pallas_call x1, Pallas kernels: 5.77 us -> 5.2 us  [on_device(): pl.pallas_call(functools.partial(project_kernel, height * nrow), grid=(he...]
where the time goes in v2:
time: 49.4 us; the launch traced here: 48.5 us
  Pallas kernels  47.9 us (97%)
  between operations  0.64 us (1%)
    pallas_call x1, Pallas kernels, on_device(): pl.pallas_call(functools.partial(kernel, nrow, ncol), out_shape=(shape((h...  42.7 us
    pallas_call x1, Pallas kernels, on_device(): pl.pallas_call(functools.partial(project_kernel, height * nrow), grid=(he...  5.2 us

profile of v2, /device:TPU:25, one launch (start us, length us, event | category | flops | bytes accessed | tf_op | source)
XLA Modules:
  0.0 48.5 jit_solution(1059292745560918763)
XLA Ops:
  0.6 42.7 %shard_map.30 = (f32[1024,128]{1,0:T(8,128)}, f32[128,128]{1,0:T(8,128)}, f32[128,512]{1,0:T(8,128)}) custom-call(f32[1024,512]{1,0:T(8,128)} %m_ref.1), custom_call_target="tpu_custom_call" | custom-call | tf_op jit(solution)/shard_map/pallas_call | solution.py:352
  43.3 5.2 %shard_map.31 = (f32[1024,512]{1,0:T(8,128)}, f32[128,512]{1,0:T(8,128)}) custom-call(f32[1024,512]{1,0:T(8,128)} %m_ref.1, f32[1024,128]{1,0:T(8,128)} %get-tuple-element.5.q_ref, f32[128,128]{1,0:T(8,128)} %get-tuple-element.6.g2_ref, f32[128,512]{1,0:T(8,128)} %get-tuple-element.7.p_ref), custom_call_target="tpu_custom_call" | custom-call | tf_op jit(solution)/shard_map/pallas_call | solution.py:380

commit v3 on v2

--- a/solution.py
+++ b/solution.py
@@ -270,6 +270,9 @@
     def _():
         load_m.wait()
         for c in range(CHUNKS // 2):
+            if c == CHUNKS // 2 - 1:
+                second.own(me, lambda: hand(1, second, 0).wait_recv())
+                second.spread()
 
             @pl.when(z == ncol - 1)
             def _():
@@ -285,8 +288,6 @@
             else:
                 sp_v[...] += term
         coeffs.start()
-        second.own(me, lambda: hand(1, second, 0).wait_recv())
-        second.spread()
 
     second.end()
     second.drain()
@@ -317,30 +318,37 @@
     return high, (x - high.astype(jnp.float32)).astype(jnp.bfloat16)
 
 
-def project_kernel(rows, m_ref, q_ref, g2_ref, p_ref, out_ref, top_ref, back_v):
-    width = m_ref.shape[1]
+def project_kernel(rows, m_ref, q_ref, g2_ref, p_ref, out_hbm, top_ref, out_v, back_v, sems):
+    height, width = m_ref.shape
+    part = height // 4
     scale = math.sqrt(rows)
     on_panel = lax.axis_index("col") == 0
-
-    @pl.when(pl.program_id(0) == 0)
-    def _():
-        g2 = g2_ref[...]
-        c = mm(g2, p_ref[...], ((1,), (0,)))
-        top_ref[...] = c / scale
-        back = mm(g2, c, ((0,), (0,)))
-        leading = jnp.where(on_panel, -scale * g2.T, back[:, :B])
-        high, low = halves(jnp.concatenate([leading, back[:, B:]], 1))
-        back_v[:B] = high
-        back_v[B : 2 * B] = high
-        back_v[2 * B :] = low
-
-    high, low = halves(q_ref[...])
-    change = jnp.dot(
-        jnp.concatenate([high, low, high], 1), back_v[...], preferred_element_type=jnp.float32
-    )
-    base = m_ref[...]
-    out_ref[:, :B] = jnp.where(on_panel, 0.0, base[:, :B]) - change[:, :B]
-    out_ref[:, B:] = base[:, B:] - change[:, B:]
+    g2 = g2_ref[...]
+    c = mm(g2, p_ref[...], ((1,), (0,)))
+    top_ref[...] = c / scale
+    back = mm(g2, c, ((0,), (0,)))
+    leading = jnp.where(on_panel, -scale * g2.T, back[:, :B])
+    high, low = halves(jnp.concatenate([leading, back[:, B:]], 1))
+    back_v[:B] = high
+    back_v[B : 2 * B] = high
+    back_v[2 * B :] = low
+
+    def store(i):
+        block = pl.ds(i * part, part)
+        return pltpu.make_async_copy(out_v.at[block], out_hbm.at[block], sems.at[i])
+
+    for i in range(4):
+        block = pl.ds(i * part, part)
+        high, low = halves(q_ref[block])
+        change = jnp.dot(
+            jnp.concatenate([high, low, high], 1), back_v[...], preferred_element_type=jnp.float32
+        )
+        base = m_ref[block]
+        out_v[block, :B] = jnp.where(on_panel, 0.0, base[:, :B]) - change[:, :B]
+        out_v[block, B:] = base[:, B:] - change[:, B:]
+        store(i).start()
+    for i in range(4):
+        store(i).wait()
 
 
 def on_device(nrow, ncol, matrix):
@@ -375,24 +383,18 @@
             collective_id=0, has_side_effects=True, vmem_limit_bytes=60 * 2**20
         ),
     )(matrix)
-    part = height // 4
     whole = pl.BlockSpec(memory_space=pltpu.VMEM)
     return pl.pallas_call(
         functools.partial(project_kernel, height * nrow),
-        grid=(height // part,),
         out_shape=(shape((height, width), f32), shape((B, width), f32)),
-        in_specs=[
-            pl.BlockSpec((part, width), lambda i: (i, 0)),
-            pl.BlockSpec((part, B), lambda i: (i, 0)),
-            whole,
-            whole,
+        in_specs=[whole] * 4,
+        out_specs=(pl.BlockSpec(memory_space=pl.ANY), whole),
+        scratch_shapes=[
+            pltpu.VMEM((height, width), f32),
+            pltpu.VMEM((3 * B, width), jnp.bfloat16),
+            dma((4,)),
         ],
-        out_specs=(
-            pl.BlockSpec((part, width), lambda i: (i, 0)),
-            pl.BlockSpec((B, width), lambda i: (0, 0)),
-        ),
-        scratch_shapes=[pltpu.VMEM((3 * B, width), jnp.bfloat16)],
-        compiler_params=pltpu.CompilerParams(vmem_limit_bytes=60 * 2**20),
+        compiler_params=pltpu.CompilerParams(vmem_limit_bytes=32 * 2**20),
     )(matrix, basis, inverse, coeffs)
 
 

time: 49.4 us -> 47.6 us (0.964)
  the two profiles are of different devices: /device:TPU:25 before, /device:TPU:17 now
where the time goes in v3:
time: 47.6 us; the launch traced here: 47.4 us
  Pallas kernels  43.9 us (92%)
  local copies, waits for them, and re-layouts  2.83 us (6%)
  between operations  0.66 us (1%)
    pallas_call x1, Pallas kernels, on_device(): pl.pallas_call(functools.partial(kernel, nrow, ncol), out_shape=(shape((h...  40.8 us
    pallas_call x1, Pallas kernels, on_device(): pl.pallas_call(functools.partial(project_kernel, height * nrow), out_shap...  3.07 us
    unnamed x8, local copies, waits for them, and re-layouts  2.83 us

profile of v3, /device:TPU:17, one launch (start us, length us, event | category | flops | bytes accessed | tf_op | source)
XLA Modules:
  0.0 47.4 jit_solution(16198427379879092280)
XLA Ops:
  0.6 0.0 copy-start
  0.6 40.8 %shard_map.30 = (f32[1024,128]{1,0:T(8,128)}, f32[128,128]{1,0:T(8,128)}, f32[128,512]{1,0:T(8,128)}) custom-call(f32[1024,512]{1,0:T(8,128)} %m_ref.1), custom_call_target="tpu_custom_call" | custom-call | tf_op jit(solution)/shard_map/pallas_call | solution.py:360
  41.4 0.0 copy-done
  41.4 0.0 copy-start.1
  41.5 1.0 %copy-done.1 = f32[1024,128]{1,0:T(8,128)S(1)} copy-done((f32[1024,128]{1,0:T(8,128)S(1)}, f32[1024,128]{1,0:T(8,128)}, u32[]{:S(2)}) %copy-start.1) | copy-done | bytes 524312
  42.5 0.0 copy-start.2
  42.5 0.9 %copy-done.2 = f32[128,512]{1,0:T(8,128)S(1)} copy-done((f32[128,512]{1,0:T(8,128)S(1)}, f32[128,512]{1,0:T(8,128)}, u32[]{:S(2)}) %copy-start.2) | copy-done | bytes 262168
  43.4 0.0 copy-start.3
  43.4 0.8 %copy-done.3 = f32[128,128]{1,0:T(8,128)S(1)} copy-done((f32[128,128]{1,0:T(8,128)S(1)}, f32[128,128]{1,0:T(8,128)}, u32[]{:S(2)}) %copy-start.3) | copy-done | bytes 65560
  44.3 3.1 %shard_map.31 = (f32[1024,512]{1,0:T(8,128)}, f32[128,512]{1,0:T(8,128)}) custom-call(f32[1024,512]{1,0:T(8,128)S(1)} %copy-done, f32[1024,128]{1,0:T(8,128)S(1)} %copy-done.1, f32[128,128]{1,0:T(8,128)S(1)} %copy-done.3, f32[128,512]{1,0:T(8,128)S(1)} %copy-done.2), custom_call_target="tpu_custom_call" | custom-call | tf_op jit(solution)/shard_map/pallas_call | solution.py:387
Async XLA Ops:
  0.6 40.8 %copy-start = (f32[1024,512]{1,0:T(8,128)S(1)}, f32[1024,512]{1,0:T(8,128)}, u32[]{:S(2)}) copy-start(f32[1024,512]{1,0:T(8,128)} %m_ref.1) | copy-start | bytes 6291460
  41.4 1.0 %copy-start.1 = (f32[1024,128]{1,0:T(8,128)S(1)}, f32[1024,128]{1,0:T(8,128)}, u32[]{:S(2)}) copy-start(f32[1024,128]{1,0:T(8,128)} %get-tuple-element.5.q_ref) | copy-start | bytes 1572868
  42.5 0.9 %copy-start.2 = (f32[128,512]{1,0:T(8,128)S(1)}, f32[128,512]{1,0:T(8,128)}, u32[]{:S(2)}) copy-start(f32[128,512]{1,0:T(8,128)} %get-tuple-element.7.p_ref) | copy-start | bytes 786436
  43.4 0.8 %copy-start.3 = (f32[128,128]{1,0:T(8,128)S(1)}, f32[128,128]{1,0:T(8,128)}, u32[]{:S(2)}) copy-start(f32[128,128]{1,0:T(8,128)} %get-tuple-element.6.g2_ref) | copy-start | bytes 196612
